TPU v7x, 128 devices: a whole 4x4x4 slice. The times are simulated.
128 devices in a mesh: bucket: 8 (over z, y_lo), dom: 16 (over y_hi, x, core).
Axes of the slice: x: 4, y: 4 (y_hi: 2, y_lo: 2; y = y_hi * 2 + y_lo), z: 4, core: 2. Of those that a mesh axis runs over, the one named last changes fastest.
Arguments:
- entity_table: float32 [16, 512, 400], P('bucket', 'dom'), may hold values from -3 to 3
- adagrad_state: float32 [16, 512], P('bucket', 'dom'), may hold values from 0.1 to 10
- relations: float32 [7424, 400], replicated, may hold values from -3 to 3
- roster: int32 [4, 8, 2], replicated, may hold values from 0 to 15, as said below
- edge_triples: int32 [128, 128, 4, 8, 3], P(('bucket', 'dom')), may hold values from 0 to 8191, as said below
- counts: int32 [128, 128, 4], P(('bucket', 'dom')), may hold values from 0 to 8, as said below
- negatives: int32 [4, 8, 16, 16, 512], P(None, 'bucket', 'dom'), may hold values from 0 to 511
Outputs:
- updated_table: float32 [16, 512, 400], P('bucket', 'dom')
- updated_state: float32 [16, 512], P('bucket', 'dom')
Inputs may be any that keep to these rules, and one draw needn't show every extreme that they name: In each step every partition 0 to 15 appears exactly once in roster[s]. `edge_triples`: for receiving device w * 16 + j and step s, every head lies in partition roster[s, w, 0] and every tail in partition roster[s, w, 1]; relation ids lie in 0 to 7423, entity ids in 0 to 8191. `counts`: in every step some receiving device gets 8 live slots from every sending device.
All inputs are finite; a program needn't handle non-finite values.
Results may differ from a plain program's by a relative error of at most 0.0003.
Values sent between devices are 32-bit elements; how exact they have to be, the bound alone decides.
No kernel may reach another device: no remote copies, remote signals or barrier semaphores. Data moves between devices by JAX's collectives and lax.ppermute only.
A program may use at most 128 MiB of HBM per device.

v0:
```python
import jax
import jax.numpy as jnp
from jax import lax
from jax.sharding import PartitionSpec as P

cubic_weight = 0.1
learn_rate = 0.05
epsilon = 1e-06


def rotate(left, right):
    half = left.shape[1] // 2
    left_re, left_im = (left[:, :half], left[:, half:])
    right_re, right_im = (right[:, :half], right[:, half:])
    return jnp.concatenate(
        [left_re * right_re - left_im * right_im, left_re * right_im + left_im * right_re], axis=1
    )


def unrotate(grad, right):
    half = grad.shape[1] // 2
    grad_re, grad_im = (grad[:, :half], grad[:, half:])
    right_re, right_im = (right[:, :half], right[:, half:])
    return jnp.concatenate(
        [grad_re * right_re + grad_im * right_im, grad_im * right_re - grad_re * right_im], axis=1
    )


def cubic_grad(values):
    half = values.shape[1] // 2
    real_part, imag_part = (values[:, :half], values[:, half:])
    modulus = jnp.sqrt(real_part * real_part + imag_part * imag_part)
    return 3.0 * cubic_weight * jnp.concatenate([modulus * real_part, modulus * imag_part], axis=1)


def contract_rows(left, right):
    return lax.dot_general(left, right, (((0,), (0,)), ((), ())), precision=lax.Precision.HIGHEST)


def slot_terms(part_src, part_dst, relations, triples, valid, negs, src_label, dst_label):
    prows = part_src.shape[0]
    head_local = triples[:, 0] - src_label * prows
    tail_local = triples[:, 2] - dst_label * prows
    head_rows = jnp.take(part_src, head_local, axis=0)
    rel_rows = jnp.take(relations, triples[:, 1], axis=0)
    tail_rows = jnp.take(part_dst, tail_local, axis=0)
    query = rotate(head_rows, rel_rows)
    scores = lax.dot_general(
        query, part_dst, (((1,), (1,)), ((), ())), precision=lax.Precision.HIGHEST
    )
    column = jnp.arange(prows, dtype=jnp.int32)
    head_hot = (head_local[:, None] == column[None, :]).astype(jnp.float32)
    tail_hot = (tail_local[:, None] == column[None, :]).astype(jnp.float32)
    nblock = negs.shape[0]
    block_counts = jnp.sum((negs[:, :, None] == column[None, None, :]).astype(jnp.float32), axis=1)
    weight = (block_counts[:, None, :] + tail_hot.reshape(nblock, -1, prows)).reshape(scores.shape)
    live = weight > 0
    top = jnp.max(jnp.where(live, scores, -1e30), axis=1, keepdims=True)
    terms = weight * jnp.exp(jnp.where(live, scores - top, -1e30))
    total = jnp.sum(terms, axis=1, keepdims=True)
    adjoint = valid[:, None] * (terms / total - tail_hot)
    grad_query = jnp.dot(adjoint, part_dst, precision=lax.Precision.HIGHEST)
    head_total = unrotate(grad_query, rel_rows) + valid[:, None] * cubic_grad(head_rows)
    tail_reg = valid[:, None] * cubic_grad(tail_rows)
    return (head_hot, tail_hot, adjoint, query, head_total, tail_reg)


def adagrad(values, state, grad):
    new_state = state + jnp.mean(grad * grad, axis=-1)
    return (values - learn_rate * grad / jnp.sqrt(new_state + epsilon)[..., None], new_state)


def select_fold(labels_all, wanted, pieces):
    flat_labels = labels_all.reshape(-1)
    piece_rows, piece_state = pieces
    matches = wanted[:, None] == flat_labels[None, :]
    rows_sum = jnp.sum(jnp.where(matches[:, :, None, None], piece_rows[None], 0.0), axis=1)
    state_sum = jnp.sum(jnp.where(matches[:, :, None], piece_state[None], 0.0), axis=1)
    return (rows_sum, state_sum)


def fetch_rows(rows_held, state_held, labels_all, wanted):
    return select_fold(
        labels_all,
        wanted,
        (
            lax.all_gather(rows_held, "bucket", axis=0, tiled=True),
            lax.all_gather(state_held, "bucket", axis=0, tiled=True),
        ),
    )


def send_home(rows_held, state_held, labels_all, wanted):
    return select_fold(
        labels_all,
        wanted,
        (
            lax.all_gather(rows_held, "bucket", axis=0, tiled=True),
            lax.all_gather(state_held, "bucket", axis=0, tiled=True),
        ),
    )


def local(entity_table, adagrad_state, relations, roster, edge_triples, counts, negatives):
    buckets = lax.axis_size("bucket")
    my_bucket = lax.axis_index("bucket")
    steps = edge_triples.shape[2]
    cap = edge_triples.shape[3]
    edge_in, count_in = (
        lax.all_to_all(edge_triples[0], ("bucket", "dom"), split_axis=0, concat_axis=0, tiled=True),
        lax.all_to_all(counts[0], ("bucket", "dom"), split_axis=0, concat_axis=0, tiled=True),
    )
    owner_labels = jnp.arange(2 * buckets, dtype=jnp.int32).reshape(buckets, 2)
    home_labels = 2 * my_bucket + jnp.arange(2, dtype=jnp.int32)
    rows_held, state_held = (entity_table, adagrad_state)
    for step_index in range(steps):
        wanted = roster[step_index, my_bucket]
        mine_rows, mine_state = fetch_rows(rows_held, state_held, owner_labels, wanted)
        full_rows = lax.all_gather(mine_rows, "dom", axis=1, tiled=True)
        triples = edge_in[:, step_index].reshape(-1, 3)
        slot_live = (
            (jnp.arange(cap, dtype=jnp.int32)[None, :] < count_in[:, step_index][:, None])
            .astype(jnp.float32)
            .reshape(-1)
        )
        head_hot, tail_hot, adjoint, query, head_total, tail_reg = slot_terms(
            full_rows[0],
            full_rows[1],
            relations,
            triples,
            slot_live,
            negatives[step_index, 0, 0],
            wanted[0],
            wanted[1],
        )
        src_side = contract_rows(head_hot, head_total)
        dst_side = contract_rows(adjoint, query) + contract_rows(tail_hot, tail_reg)
        shares = lax.psum_scatter(
            jnp.concatenate([src_side, dst_side], axis=1), "dom", scatter_dimension=0, tiled=True
        )
        width = mine_rows.shape[2]
        grads = jnp.stack([shares[:, :width], shares[:, width:]])
        new_rows, new_state = adagrad(mine_rows, mine_state, grads)
        rows_held, state_held = send_home(new_rows, new_state, roster[step_index], home_labels)
    return (rows_held, state_held)


def solution(mesh):
    in_specs = (
        P("bucket", "dom", None),
        P("bucket", "dom"),
        P(),
        P(),
        P(("bucket", "dom"), None, None, None, None),
        P(("bucket", "dom"), None, None),
        P(None, "bucket", "dom", None, None),
    )
    out_specs = (P("bucket", "dom", None), P("bucket", "dom"))
    return jax.shard_map(local, mesh=mesh, in_specs=in_specs, out_specs=out_specs, check_vma=False)
```

profile of v0, /device:TPU:2, one launch (start us, length us, event | category | flops | bytes accessed | tf_op | source)
XLA Modules:
  0.0 983.3 jit_solution(17356970910296015559)
XLA Ops:
  7.2 34.7 %all_gather.60 = f32[16,32,400]{2,1,0:T(8,128)S(1)} all-gather(f32[2,32,400]{2,1,0:T(8,128)} %param.11), channel_id=1, replica_groups=mesh['bucket'=8,'dom'=16] {'bucket'}, dimensions={0}, use_global_device_ids=true | all-gather | bytes 921600 | tf_op jit(solution)/shard_map/all_gather | solution.py:87
  45.9 8.8 all-to-all-start.1
  55.3 4.7 convert_reduce_fusion.2
  63.0 14.1 %copy.266 = f32[7424,400]{1,0:T(8,128)} copy(f32[7424,400]{0,1:T(8,128)} %param.13) | data formatting | bytes 23756800 | tf_op args[2]
  79.3 9.8 all-to-all-start
  90.3 14.7 %all-to-all-done = s32[128,4,8,3]{2,1,3,0:T(4,128)S(1)} async-done(((s32[128,4,8,3]{2,1,3,0:T(4,128)}), s32[128,4,8,3]{2,1,3,0:T(4,128)S(1)}, u32[]{:S(2)}, u32[]{:S(2)}) %all-to-all-start) | async-done | bytes 49184 | tf_op jit(solution)/shard_map/all_to_all | solution.py:110
  106.5 9.3 gather_fusion.1
  118.2 2.8 broadcast_select_fusion.10
  121.0 4.0 fusion.147
  126.1 4.9 gather_fusion
  130.9 2.9 copy.265
  138.2 3.9 select_reduce_fusion.10
  142.9 4.2 fusion.46
  147.1 4.4 fusion.94
  151.5 4.9 gather_fusion.2
  167.9 15.3 %all-gather = f32[8,2,32]{2,1,0:T(2,128)S(1)} all-gather(f32[1,2,32]{2,1,0:T(2,128)S(1)} %bitcast.199), channel_id=1, replica_groups=mesh['bucket'=8,'dom'=16] {'bucket'}, dimensions={0}, use_global_device_ids=true | all-gather | bytes 2304 | tf_op jit(solution)/shard_map/all_gather | solution.py:88
  184.0 49.1 %reduce-scatter.13.cloned.1.call-done = f32[32,800]{1,0:T(8,128)} async-done(((f32[512,800]{1,0:T(8,128)}), f32[32,800]{1,0:T(8,128)}) %reduce-scatter.13.cloned.1.call-update) | async-done | bytes 102416 | tf_op jit(solution)/shard_map/reduce_scatter | solution.py:138
  234.9 33.0 %all_gather.63 = f32[16,32,400]{2,1,0:T(8,128)S(1)} all-gather(f32[2,32,400]{2,1,0:T(8,128)S(1)} %divide_subtract_fusion.3), channel_id=1, replica_groups=mesh['bucket'=8,'dom'=16] {'bucket'}, dimensions={0}, use_global_device_ids=true | all-gather | bytes 921600 | tf_op jit(solution)/shard_map/all_gather | solution.py:98
  268.1 32.0 %all_gather.64 = f32[16,32,400]{2,1,0:T(8,128)S(1)} all-gather(f32[2,32,400]{2,1,0:T(8,128)S(1)} %select_reduce_fusion.9), channel_id=1, replica_groups=mesh['bucket'=8,'dom'=16] {'bucket'}, dimensions={0}, use_global_device_ids=true | all-gather | bytes 921600 | tf_op jit(solution)/shard_map/all_gather | solution.py:87
  306.6 10.8 %gather_fusion.4 = f32[1024,400]{1,0:T(8,128)} fusion(f32[7424,400]{1,0:T(8,128)} %copy.266, s32[1024]{0:T(1024)S(1)} %fusion.108), kind=kCustom, calls=%fused_computation.9.clone | custom fusion | bytes 3280896 | tf_op jit(solution)/shard_map/jit(_take)/gather | solution.py:45
  320.2 2.8 broadcast_select_fusion.7
  323.0 25.1 %all-gather.15.cloned.1.call-done = f32[2,512,400]{2,0,1:T(2,128)} async-done(((f32[2,32,400]{2,0,1:T(2,128)}), f32[2,512,400]{2,0,1:T(2,128)}) %all-gather.15.cloned.1.call-update) | async-done | bytes 1638416 | tf_op jit(solution)/shard_map/all_gather | solution.py:119
  348.0 5.0 fusion.146
  353.1 4.9 gather_fusion.3
  358.0 3.1 copy.276
  366.1 3.8 select_reduce_fusion.7
  370.6 4.2 fusion.44
  374.8 4.4 fusion.91
  379.2 3.5 gather_fusion.5
  394.8 18.1 %all-gather.1 = f32[8,2,32]{2,1,0:T(2,128)S(1)} all-gather(f32[1,2,32]{2,1,0:T(2,128)S(1)} %copy-done.42), channel_id=1, replica_groups=mesh['bucket'=8,'dom'=16] {'bucket'}, dimensions={0}, use_global_device_ids=true | all-gather | bytes 2304 | tf_op jit(solution)/shard_map/all_gather | solution.py:99
  412.9 15.1 %all-gather.2 = f32[8,2,32]{2,1,0:T(2,128)S(1)} all-gather(f32[1,2,32]{2,1,0:T(2,128)S(1)} %bitcast.196), channel_id=1, replica_groups=mesh['bucket'=8,'dom'=16] {'bucket'}, dimensions={0}, use_global_device_ids=true | all-gather | bytes 2304 | tf_op jit(solution)/shard_map/all_gather | solution.py:88
  428.1 35.2 %reduce-scatter.15.cloned.1.call-done = f32[32,800]{1,0:T(8,128)} async-done(((f32[512,800]{1,0:T(8,128)}), f32[32,800]{1,0:T(8,128)}) %reduce-scatter.15.cloned.1.call-update) | async-done | bytes 102416 | tf_op jit(solution)/shard_map/reduce_scatter | solution.py:138
  464.6 32.9 %all_gather.68 = f32[16,32,400]{2,1,0:T(8,128)S(1)} all-gather(f32[2,32,400]{2,1,0:T(8,128)S(1)} %divide_subtract_fusion.2), channel_id=1, replica_groups=mesh['bucket'=8,'dom'=16] {'bucket'}, dimensions={0}, use_global_device_ids=true | all-gather | bytes 921600 | tf_op jit(solution)/shard_map/all_gather | solution.py:98
  497.8 31.9 %all_gather.69 = f32[16,32,400]{2,1,0:T(8,128)S(1)} all-gather(f32[2,32,400]{2,1,0:T(8,128)S(1)} %select_reduce_fusion.6), channel_id=1, replica_groups=mesh['bucket'=8,'dom'=16] {'bucket'}, dimensions={0}, use_global_device_ids=true | all-gather | bytes 921600 | tf_op jit(solution)/shard_map/all_gather | solution.py:87
  532.6 4.7 convert_reduce_fusion
  541.5 10.6 %gather_fusion.7 = f32[1024,400]{1,0:T(8,128)} fusion(f32[7424,400]{1,0:T(8,128)} %copy.266, s32[1024]{0:T(1024)S(1)} %fusion.111), kind=kCustom, calls=%fused_computation.10.clone | custom fusion | bytes 3280896 | tf_op jit(solution)/shard_map/jit(_take)/gather | solution.py:45
  555.0 2.8 broadcast_select_fusion.4
  557.8 20.0 %all-gather.17.cloned.1.call-done = f32[2,512,400]{2,0,1:T(2,128)} async-done(((f32[2,32,400]{2,0,1:T(2,128)}), f32[2,512,400]{2,0,1:T(2,128)}) %all-gather.17.cloned.1.call-update) | async-done | bytes 1638416 | tf_op jit(solution)/shard_map/all_gather | solution.py:119
  577.8 5.0 fusion.145
  582.8 4.9 gather_fusion.6
  587.7 2.9 copy.287
  595.6 3.8 select_reduce_fusion.4
  600.2 4.2 fusion.42
  604.3 4.4 fusion.88
  608.7 3.5 gather_fusion.8
  624.5 18.1 %all-gather.3 = f32[8,2,32]{2,1,0:T(2,128)S(1)} all-gather(f32[1,2,32]{2,1,0:T(2,128)S(1)} %get-tuple-element.114), channel_id=1, replica_groups=mesh['bucket'=8,'dom'=16] {'bucket'}, dimensions={0}, use_global_device_ids=true | all-gather | bytes 2304 | tf_op jit(solution)/shard_map/all_gather | solution.py:99
  642.7 15.1 %all-gather.4 = f32[8,2,32]{2,1,0:T(2,128)S(1)} all-gather(f32[1,2,32]{2,1,0:T(2,128)S(1)} %bitcast.197), channel_id=1, replica_groups=mesh['bucket'=8,'dom'=16] {'bucket'}, dimensions={0}, use_global_device_ids=true | all-gather | bytes 2304 | tf_op jit(solution)/shard_map/all_gather | solution.py:88
  657.9 35.3 %reduce-scatter.17.cloned.1.call-done = f32[32,800]{1,0:T(8,128)} async-done(((f32[512,800]{1,0:T(8,128)}), f32[32,800]{1,0:T(8,128)}) %reduce-scatter.17.cloned.1.call-update) | async-done | bytes 102416 | tf_op jit(solution)/shard_map/reduce_scatter | solution.py:138
  694.4 32.9 %all_gather.73 = f32[16,32,400]{2,1,0:T(8,128)S(1)} all-gather(f32[2,32,400]{2,1,0:T(8,128)S(1)} %divide_subtract_fusion.1), channel_id=1, replica_groups=mesh['bucket'=8,'dom'=16] {'bucket'}, dimensions={0}, use_global_device_ids=true | all-gather | bytes 921600 | tf_op jit(solution)/shard_map/all_gather | solution.py:98
  727.5 32.1 %all_gather.74 = f32[16,32,400]{2,1,0:T(8,128)S(1)} all-gather(f32[2,32,400]{2,1,0:T(8,128)S(1)} %select_reduce_fusion.3), channel_id=1, replica_groups=mesh['bucket'=8,'dom'=16] {'bucket'}, dimensions={0}, use_global_device_ids=true | all-gather | bytes 921600 | tf_op jit(solution)/shard_map/all_gather | solution.py:87
  766.0 10.8 %gather_fusion.10 = f32[1024,400]{1,0:T(8,128)} fusion(f32[7424,400]{1,0:T(8,128)} %copy.266, s32[1024]{0:T(1024)S(1)} %fusion.114), kind=kCustom, calls=%fused_computation.11.clone | custom fusion | bytes 3280896 | tf_op jit(solution)/shard_map/jit(_take)/gather | solution.py:45
  782.4 25.0 %all-gather.19.cloned.1.call-done = f32[2,512,400]{2,0,1:T(2,128)} async-done(((f32[2,32,400]{2,0,1:T(2,128)}), f32[2,512,400]{2,0,1:T(2,128)}) %all-gather.19.cloned.1.call-update) | async-done | bytes 1638416 | tf_op jit(solution)/shard_map/all_gather | solution.py:119
  807.4 5.0 fusion.144
  812.5 4.9 gather_fusion.9
  817.4 3.0 copy.298
  825.3 3.8 select_reduce_fusion.1
  829.9 4.2 fusion.40
  834.1 4.4 fusion.85
  838.4 3.5 gather_fusion.11
  854.0 18.1 %all-gather.5 = f32[8,2,32]{2,1,0:T(2,128)S(1)} all-gather(f32[1,2,32]{2,1,0:T(2,128)S(1)} %get-tuple-element.112), channel_id=1, replica_groups=mesh['bucket'=8,'dom'=16] {'bucket'}, dimensions={0}, use_global_device_ids=true | all-gather | bytes 2304 | tf_op jit(solution)/shard_map/all_gather | solution.py:99
  872.1 15.1 %all-gather.6 = f32[8,2,32]{2,1,0:T(2,128)S(1)} all-gather(f32[1,2,32]{2,1,0:T(2,128)S(1)} %bitcast.198), channel_id=1, replica_groups=mesh['bucket'=8,'dom'=16] {'bucket'}, dimensions={0}, use_global_device_ids=true | all-gather | bytes 2304 | tf_op jit(solution)/shard_map/all_gather | solution.py:88
  887.3 35.4 %reduce-scatter.19.cloned.1.call-done = f32[32,800]{1,0:T(8,128)} async-done(((f32[512,800]{1,0:T(8,128)}), f32[32,800]{1,0:T(8,128)}) %reduce-scatter.19.cloned.1.call-update) | async-done | bytes 102416 | tf_op jit(solution)/shard_map/reduce_scatter | solution.py:138
  923.9 32.9 %all_gather.78 = f32[16,32,400]{2,1,0:T(8,128)S(1)} all-gather(f32[2,32,400]{2,1,0:T(8,128)S(1)} %divide_subtract_fusion), channel_id=1, replica_groups=mesh['bucket'=8,'dom'=16] {'bucket'}, dimensions={0}, use_global_device_ids=true | all-gather | bytes 921600 | tf_op jit(solution)/shard_map/all_gather | solution.py:98
  956.8 17.9 %all-gather.7 = f32[8,2,32]{2,1,0:T(2,128)S(1)} all-gather(f32[1,2,32]{2,1,0:T(2,128)S(1)} %get-tuple-element.110), channel_id=1, replica_groups=mesh['bucket'=8,'dom'=16] {'bucket'}, dimensions={0}, use_global_device_ids=true | all-gather | bytes 2304 | tf_op jit(solution)/shard_map/all_gather | solution.py:99
  (307 shorter events, 120.1 us)
Async XLA Ops:
  7.2 38.0 %copy-start.49 = (s32[1,128,4]{1,2,0:T(4,128)S(1)}, s32[1,128,4]{1,2,0:T(4,128)}, u32[]{:S(2)}) copy-start(s32[1,128,4]{1,2,0:T(4,128)} %param.16) | copy-start | bytes 6148
  7.2 47.5 %copy-start.31 = (s32[4,1,1,16,512]{4,3,2,1,0:T(8,128)S(1)}, s32[4,1,1,16,512]{4,3,2,1,0:T(8,128)}, u32[]{:S(2)}) copy-start(s32[4,1,1,16,512]{4,3,2,1,0:T(8,128)} %param.17) | copy-start | bytes 393220
  7.2 53.4 %copy-start.33 = (s32[1,128,4,8,3]{1,3,4,2,0:T(8,128)S(1)}, s32[1,128,4,8,3]{1,3,4,2,0:T(8,128)}, u32[]{:S(2)}) copy-start(s32[1,128,4,8,3]{1,3,4,2,0:T(8,128)} %param.15) | copy-start | bytes 147460
  7.2 113.8 %all-gather.13.cloned.1.call-start = ((), (), s32[]{:S(2)}) async-start(), calls=%async_computation.6 | async-start | bytes 2228224 | tf_op jit(solution)/shard_map/all_gather | solution.py:119
  44.1 1.8 copy-start.45
  45.9 33.4 %all-to-all-start.1 = ((s32[128,1,4]{2,1,0:T(1,128)}), s32[128,1,4]{2,1,0:T(1,128)S(1)}, u32[]{:S(2)}, u32[]{:S(2)}) async-start(s32[128,1,4]{2,1,0:T(1,128)} %bitcast.3), calls=%async_computation.1 | async-start | bytes 131072 | tf_op jit(solution)/shard_map/all_to_all | solution.py:111
  79.3 25.7 %all-to-all-start = ((s32[128,4,8,3]{2,1,3,0:T(4,128)}), s32[128,4,8,3]{2,1,3,0:T(4,128)S(1)}, u32[]{:S(2)}, u32[]{:S(2)}) async-start(s32[128,4,8,3]{2,1,3,0:T(4,128)} %bitcast), calls=%async_computation | async-start | bytes 1572864 | tf_op jit(solution)/shard_map/all_to_all | solution.py:110
  89.0 144.2 %reduce-scatter.13.cloned.1.call-start = ((), (), s32[]{:S(2)}) async-start(), calls=%async_computation.10 | async-start | bytes 1949696 | tf_op jit(solution)/shard_map/reduce_scatter | solution.py:138
  89.3 17.2 %copy-start.35 = (s32[128]{0:T(128)}, s32[128]{0:T(128)S(1)}, u32[]{:S(2)}) copy-start(s32[128]{0:T(128)S(1)} %get-tuple-element.6) | copy-start | bytes 1540
  133.9 1.9 copy-start.1
  135.8 1.9 copy-start
  135.8 2.4 copy-start.12
  159.2 1.4 copy-start.16
  160.6 1.1 copy-start.54
  161.0 2.5 copy-start.20
  161.0 2.5 copy-start.21
  165.4 1.8 copy-start.34
  165.4 2.5 copy-start.50
  165.5 17.8 %copy-start.46 = (pred[2,16]{1,0:T(4,128)(4,1)S(1)}, pred[2,16]{1,0:T(4,128)(4,1)}, u32[]{:S(2)}) copy-start(pred[2,16]{1,0:T(4,128)(4,1)} %copy-done.45) | copy-start | bytes 100
  165.5 17.9 %copy-start.53 = (s32[2]{0:T(128)S(1)}, s32[2]{0:T(128)}, u32[]{:S(2)}) copy-start(s32[2]{0:T(128)} %get-tuple-element.104) | copy-start | bytes 28
  167.2 180.8 %all-gather.15.cloned.1.call-start = ((), (), s32[]{:S(2)}) async-start(), calls=%async_computation.7 | async-start | bytes 2228224 | tf_op jit(solution)/shard_map/all_gather | solution.py:119
  183.4 116.8 %copy-start.47 = (pred[2,16]{1,0:T(4,128)(4,1)}, pred[2,16]{1,0:T(4,128)(4,1)S(1)}, u32[]{:S(2)}) copy-start(pred[2,16]{1,0:T(4,128)(4,1)S(1)} %iota_compare_fusion.33) | copy-start | bytes 100
  184.0 116.1 %copy-start.39 = (pred[2,16]{1,0:T(4,128)(4,1)}, pred[2,16]{1,0:T(4,128)(4,1)S(1)}, u32[]{:S(2)}) copy-start(pred[2,16]{1,0:T(4,128)(4,1)S(1)} %get-tuple-element.129) | copy-start | bytes 100
  301.2 162.2 %reduce-scatter.15.cloned.1.call-start = ((), (), s32[]{:S(2)}) async-start(), calls=%async_computation.11 | async-start | bytes 1949696 | tf_op jit(solution)/shard_map/reduce_scatter | solution.py:138
  304.1 2.0 copy-start.36
  304.1 2.3 copy-start.30
  361.1 1.7 copy-start.13
  362.9 1.4 copy-start.2
  364.3 1.8 copy-start.8
  386.2 1.4 copy-start.3
  386.2 1.9 copy-start.17
  388.5 2.4 copy-start.22
  388.6 2.4 copy-start.23
  392.9 1.8 copy-start.52
  392.9 1.9 copy-start.42
  392.9 19.9 %copy-start.40 = (pred[2,16]{1,0:T(4,128)(4,1)S(1)}, pred[2,16]{1,0:T(4,128)(4,1)}, u32[]{:S(2)}) copy-start(pred[2,16]{1,0:T(4,128)(4,1)} %copy-done.39) | copy-start | bytes 100
  392.9 35.1 %copy-start.48 = (pred[2,16]{1,0:T(4,128)(4,1)S(1)}, pred[2,16]{1,0:T(4,128)(4,1)}, u32[]{:S(2)}) copy-start(pred[2,16]{1,0:T(4,128)(4,1)} %copy-done.47) | copy-start | bytes 100
  394.6 102.9 %copy-start.38 = (pred[2,16]{1,0:T(4,128)(4,1)S(1)}, pred[2,16]{1,0:T(4,128)(4,1)}, u32[]{:S(2)}) copy-start(pred[2,16]{1,0:T(4,128)(4,1)} %get-tuple-element.128) | copy-start | bytes 100
  394.6 183.1 %all-gather.17.cloned.1.call-start = ((), (), s32[]{:S(2)}) async-start(), calls=%async_computation.8 | async-start | bytes 2228224 | tf_op jit(solution)/shard_map/all_gather | solution.py:119
  497.5 33.2 %copy-start.43 = (s32[1,1,2]{1,2,0:T(2,128)S(1)}, s32[1,1,2]{1,2,0:T(2,128)}, u32[]{:S(2)}) copy-start(s32[1,1,2]{1,2,0:T(2,128)} %get-tuple-element.11) | copy-start | bytes 28
  497.5 33.2 %copy-start.44 = (s32[1,1,2]{1,2,0:T(2,128)S(1)}, s32[1,1,2]{1,2,0:T(2,128)}, u32[]{:S(2)}) copy-start(s32[1,1,2]{1,2,0:T(2,128)} %get-tuple-element.107) | copy-start | bytes 28
  497.5 35.1 %copy-start.32 = (s32[16,512]{1,0:T(8,128)S(1)}, s32[16,512]{1,0:T(8,128)}, u32[]{:S(2)}) copy-start(s32[16,512]{1,0:T(8,128)} %get-tuple-element.79) | copy-start | bytes 98308
  530.7 162.5 %reduce-scatter.17.cloned.1.call-start = ((), (), s32[]{:S(2)}) async-start(), calls=%async_computation.12 | async-start | bytes 1949696 | tf_op jit(solution)/shard_map/reduce_scatter | solution.py:138
  538.9 2.4 copy-start.29
  590.7 1.7 copy-start.14
  592.4 1.4 copy-start.4
  593.8 1.8 copy-start.9
  615.9 1.4 copy-start.5
  615.9 1.9 copy-start.18
  617.8 1.1 copy-start.56
  618.3 2.4 copy-start.24
  618.3 2.4 copy-start.25
  622.6 1.8 copy-start.51
  624.3 103.0 %copy-start.37 = (pred[2,16]{1,0:T(4,128)(4,1)S(1)}, pred[2,16]{1,0:T(4,128)(4,1)}, u32[]{:S(2)}) copy-start(pred[2,16]{1,0:T(4,128)(4,1)} %get-tuple-element.127) | copy-start | bytes 100
  624.4 183.1 %all-gather.19.cloned.1.call-start = ((), (), s32[]{:S(2)}) async-start(), calls=%async_computation.9 | async-start | bytes 2228224 | tf_op jit(solution)/shard_map/all_gather | solution.py:119
  760.7 162.0 %reduce-scatter.19.cloned.1.call-start = ((), (), s32[]{:S(2)}) async-start(), calls=%async_computation.13 | async-start | bytes 1949696 | tf_op jit(solution)/shard_map/reduce_scatter | solution.py:138
  763.6 2.2 copy-start.28
  820.3 1.7 copy-start.15
  822.1 1.4 copy-start.6
  823.5 1.8 copy-start.10
  845.5 1.4 copy-start.7
  845.5 1.9 copy-start.19
  847.9 2.4 copy-start.26
  847.9 2.4 copy-start.27
  (4 other events, 4.0 us)
Sparse Core Ops, SparseCore 0:
  45.2 49.2 all-gather.12
  167.3 65.8 reduce-scatter.12
  301.3 46.6 all-gather.14
  394.8 68.5 reduce-scatter.14
  530.8 46.9 all-gather.16
  624.5 68.6 reduce-scatter.16
  760.8 46.5 all-gather.18
  854.1 68.5 reduce-scatter.18
where the time goes:
time: 992 us; the launch traced here: 983 us
  blocking collectives  395 us (40%)
  waiting for transfers between devices  240 us (24%)
  local copies, waits for them, and re-layouts  196 us (20%)
  matrix products  63.5 us (6%)
  other arithmetic  49 us (5%)
  between operations  20.7 us (2%)
  starting transfers between devices  18.9 us (2%)
    reduce_scatter x4, waiting for transfers between devices, local(): lax.psum_scatter(jnp.concatenate([src_side, dst_side], axis=1), 'dom', sc...  155 us
    all_gather x4, blocking collectives, send_home(): lax.all_gather(rows_held, 'bucket', axis=0, tiled=True)  132 us
    all_gather x4, blocking collectives, fetch_rows(): lax.all_gather(rows_held, 'bucket', axis=0, tiled=True)  131 us
    all_gather x4, blocking collectives, send_home(): lax.all_gather(state_held, 'bucket', axis=0, tiled=True)  72.1 us
    all_gather x4, waiting for transfers between devices, local(): full_rows = lax.all_gather(mine_rows, 'dom', axis=1, tiled=True)  70 us
    all_gather x4, blocking collectives, fetch_rows(): lax.all_gather(state_held, 'bucket', axis=0, tiled=True)  60.6 us
    gather x8, local copies, waits for them, and re-layouts, slot_terms(): rel_rows = jnp.take(relations, triples[:, 1], axis=0)  51.5 us
    unnamed x129, local copies, waits for them, and re-layouts  42.7 us
  transfers between devices with their start and end apart: 10, of which 8 were waited for; matrix products, arithmetic and copies ran while one was open for 11% of the time, Pallas kernels for 0%

commit v1 on v0

--- a/solution.py
+++ b/solution.py
@@ -6,6 +6,11 @@
 cubic_weight = 0.1
 learn_rate = 0.05
 epsilon = 1e-06
+
+
+def all_by_exchange(x, axis, along):
+    sent = jnp.stack([x] * lax.axis_size(axis))
+    return jnp.concatenate(lax.all_to_all(sent, axis, 0, 0), axis=along)
 
 
 def rotate(left, right):
@@ -84,7 +89,7 @@
         labels_all,
         wanted,
         (
-            lax.all_gather(rows_held, "bucket", axis=0, tiled=True),
+            all_by_exchange(rows_held, "bucket", 0),
             lax.all_gather(state_held, "bucket", axis=0, tiled=True),
         ),
     )

time: 992 us -> 929 us (0.936)
  blocking collectives: 395 us -> 264 us
  waiting for transfers between devices: 240 us -> 286 us
  starting transfers between devices: 18.9 us -> 35.8 us
    all_gather x4 -> x0, blocking collectives: 131 us -> none  [fetch_rows(): lax.all_gather(rows_held, 'bucket', axis=0, tiled=True)]
    all_to_all x0 -> x4, waiting for transfers between devices: none -> 47.2 us  [all_by_exchange(): return jnp.concatenate(lax.all_to_all(sent, axis, 0, 0), axis=along)]
    all_to_all x0 -> x4, starting transfers between devices: none -> 18.6 us  [all_by_exchange(): return jnp.concatenate(lax.all_to_all(sent, axis, 0, 0), axis=along)]
    unnamed x129 -> x125, local copies, waits for them, and re-layouts: 42.7 us -> 42.7 us
  transfers between devices with their start and end apart: 10 -> 14, of which waited for: 8 -> 12; matrix products, arithmetic and copies ran while one was open for 11% -> 12% of each run, Pallas kernels for 0% -> 0%
where the time goes in v1:
time: 929 us; the launch traced here: 920 us
  waiting for transfers between devices  286 us (31%)
  blocking collectives  264 us (28%)
  local copies, waits for them, and re-layouts  201 us (22%)
  matrix products  63.5 us (7%)
  other arithmetic  49.2 us (5%)
  starting transfers between devices  35.8 us (4%)
  between operations  20.7 us (2%)
    reduce_scatter x4, waiting for transfers between devices, local(): lax.psum_scatter(jnp.concatenate([src_side, dst_side], axis=1), 'dom', sc...  156 us
    all_gather x4, blocking collectives, send_home(): lax.all_gather(rows_held, 'bucket', axis=0, tiled=True)  131 us
    all_gather x4, blocking collectives, send_home(): lax.all_gather(state_held, 'bucket', axis=0, tiled=True)  72.1 us
    all_gather x4, waiting for transfers between devices, local(): full_rows = lax.all_gather(mine_rows, 'dom', axis=1, tiled=True)  66.6 us
    all_gather x4, blocking collectives, fetch_rows(): lax.all_gather(state_held, 'bucket', axis=0, tiled=True)  60.5 us
    gather x8, local copies, waits for them, and re-layouts, slot_terms(): rel_rows = jnp.take(relations, triples[:, 1], axis=0)  51.6 us
    all_to_all x4, waiting for transfers between devices, all_by_exchange(): return jnp.concatenate(lax.all_to_all(sent, axis, 0, 0), axis=along)  47.2 us
    unnamed x125, local copies, waits for them, and re-layouts  42.7 us
  transfers between devices with their start and end apart: 14, of which 12 were waited for; matrix products, arithmetic and copies ran while one was open for 12% of the time, Pallas kernels for 0%

profile of v1, /device:TPU:2, one launch (start us, length us, event | category | flops | bytes accessed | tf_op | source)
XLA Modules:
  0.0 920.1 jit_solution(6599666799235193215)
XLA Ops:
  9.2 6.5 all-to-all-start
  18.4 12.9 %all-to-all-done = f32[8,2,32,400]{3,2,1,0:T(8,128)S(1)} async-done(((f32[8,2,32,400]{3,2,1,0:T(8,128)}), f32[8,2,32,400]{3,2,1,0:T(8,128)S(1)}, u32[]{:S(2)}, u32[]{:S(2)}) %all-to-all-start) | async-done | bytes 819232 | tf_op jit(solution)/shard_map/all_to_all | solution.py:13
  31.4 7.1 all-to-all-start.2
  39.5 4.7 convert_reduce_fusion.2
  47.3 14.2 %copy.266 = f32[7424,400]{1,0:T(8,128)} copy(f32[7424,400]{0,1:T(8,128)} %param.13) | data formatting | bytes 23756800 | tf_op args[2]
  63.5 9.8 %all-to-all-start.1 = ((s32[128,4,8,3]{2,1,3,0:T(4,128)}), s32[128,4,8,3]{2,1,3,0:T(4,128)S(1)}, u32[]{:S(2)}, u32[]{:S(2)}) async-start(s32[128,4,8,3]{2,1,3,0:T(4,128)} %bitcast.1), calls=%async_computation.1 | async-start | bytes 1572864 | tf_op jit(solution)/shard_map/all_to_all | solution.py:115
  75.1 15.7 %all-to-all-done.1 = s32[128,4,8,3]{2,1,3,0:T(4,128)S(1)} async-done(((s32[128,4,8,3]{2,1,3,0:T(4,128)}), s32[128,4,8,3]{2,1,3,0:T(4,128)S(1)}, u32[]{:S(2)}, u32[]{:S(2)}) %all-to-all-start.1) | async-done | bytes 49184 | tf_op jit(solution)/shard_map/all_to_all | solution.py:115
  92.4 9.5 %gather_fusion.1 = f32[1024,400]{1,0:T(8,128)S(1)} fusion(f32[7424,400]{1,0:T(8,128)} %copy.266, s32[1024]{0:T(1024)S(1)} %fusion.105), kind=kCustom, calls=%fused_computation.1.clone | custom fusion | bytes 3280896 | tf_op jit(solution)/shard_map/jit(_take)/gather | solution.py:50
  107.1 4.0 fusion.147
  112.1 4.9 gather_fusion
  124.3 3.8 select_reduce_fusion.10
  129.0 4.2 fusion.46
  133.1 4.4 fusion.94
  137.5 4.9 gather_fusion.2
  153.9 15.2 %all-gather = f32[8,2,32]{2,1,0:T(2,128)S(1)} all-gather(f32[1,2,32]{2,1,0:T(2,128)S(1)} %bitcast.207), channel_id=1, replica_groups=mesh['bucket'=8,'dom'=16] {'bucket'}, dimensions={0}, use_global_device_ids=true | all-gather | bytes 2304 | tf_op jit(solution)/shard_map/all_gather | solution.py:93
  169.8 50.1 %reduce-scatter.13.cloned.1.call-done = f32[32,800]{1,0:T(8,128)} async-done(((f32[512,800]{1,0:T(8,128)}), f32[32,800]{1,0:T(8,128)}) %reduce-scatter.13.cloned.1.call-update) | async-done | bytes 102416 | tf_op jit(solution)/shard_map/reduce_scatter | solution.py:143
  221.7 32.8 %all_gather.50 = f32[16,32,400]{2,1,0:T(8,128)S(1)} all-gather(f32[2,32,400]{2,1,0:T(8,128)S(1)} %divide_subtract_fusion.3), channel_id=1, replica_groups=mesh['bucket'=8,'dom'=16] {'bucket'}, dimensions={0}, use_global_device_ids=true | all-gather | bytes 921600 | tf_op jit(solution)/shard_map/all_gather | solution.py:103
  255.8 4.2 all-to-all-start.3
  260.1 11.4 %all-to-all-done.3 = f32[8,2,32,400]{3,2,1,0:T(8,128)S(1)} async-done(((f32[8,2,32,400]{3,2,1,0:T(8,128)}), f32[8,2,32,400]{3,2,1,0:T(8,128)S(1)}, u32[]{:S(2)}, u32[]{:S(2)}) %all-to-all-start.3) | async-done | bytes 819232 | tf_op jit(solution)/shard_map/all_to_all | solution.py:13
  277.9 10.7 %gather_fusion.4 = f32[1024,400]{1,0:T(8,128)} fusion(f32[7424,400]{1,0:T(8,128)} %copy.266, s32[1024]{0:T(1024)S(1)} %fusion.108), kind=kCustom, calls=%fused_computation.9.clone | custom fusion | bytes 3280896 | tf_op jit(solution)/shard_map/jit(_take)/gather | solution.py:50
  294.3 23.7 %all-gather.15.cloned.1.call-done = f32[2,512,400]{2,0,1:T(2,128)} async-done(((f32[2,32,400]{2,0,1:T(2,128)}), f32[2,512,400]{2,0,1:T(2,128)}) %all-gather.15.cloned.1.call-update) | async-done | bytes 1638416 | tf_op jit(solution)/shard_map/all_gather | solution.py:124
  318.1 5.0 fusion.146
  323.1 4.9 gather_fusion.3
  328.0 3.1 copy.276
  336.1 3.8 select_reduce_fusion.7
  340.7 4.2 fusion.44
  344.9 4.4 fusion.91
  349.3 3.5 gather_fusion.5
  364.7 18.1 %all-gather.1 = f32[8,2,32]{2,1,0:T(2,128)S(1)} all-gather(f32[1,2,32]{2,1,0:T(2,128)S(1)} %copy-done.42), channel_id=1, replica_groups=mesh['bucket'=8,'dom'=16] {'bucket'}, dimensions={0}, use_global_device_ids=true | all-gather | bytes 2304 | tf_op jit(solution)/shard_map/all_gather | solution.py:104
  382.9 15.1 %all-gather.2 = f32[8,2,32]{2,1,0:T(2,128)S(1)} all-gather(f32[1,2,32]{2,1,0:T(2,128)S(1)} %bitcast.204), channel_id=1, replica_groups=mesh['bucket'=8,'dom'=16] {'bucket'}, dimensions={0}, use_global_device_ids=true | all-gather | bytes 2304 | tf_op jit(solution)/shard_map/all_gather | solution.py:93
  398.1 35.4 %reduce-scatter.15.cloned.1.call-done = f32[32,800]{1,0:T(8,128)} async-done(((f32[512,800]{1,0:T(8,128)}), f32[32,800]{1,0:T(8,128)}) %reduce-scatter.15.cloned.1.call-update) | async-done | bytes 102416 | tf_op jit(solution)/shard_map/reduce_scatter | solution.py:143
  434.6 32.7 %all_gather.54 = f32[16,32,400]{2,1,0:T(8,128)S(1)} all-gather(f32[2,32,400]{2,1,0:T(8,128)S(1)} %divide_subtract_fusion.2), channel_id=1, replica_groups=mesh['bucket'=8,'dom'=16] {'bucket'}, dimensions={0}, use_global_device_ids=true | all-gather | bytes 921600 | tf_op jit(solution)/shard_map/all_gather | solution.py:103
  468.7 4.1 all-to-all-start.4
  472.9 11.4 %all-to-all-done.4 = f32[8,2,32,400]{3,2,1,0:T(8,128)S(1)} async-done(((f32[8,2,32,400]{3,2,1,0:T(8,128)}), f32[8,2,32,400]{3,2,1,0:T(8,128)S(1)}, u32[]{:S(2)}, u32[]{:S(2)}) %all-to-all-start.4) | async-done | bytes 819232 | tf_op jit(solution)/shard_map/all_to_all | solution.py:13
  487.4 4.7 convert_reduce_fusion
  496.3 10.6 %gather_fusion.7 = f32[1024,400]{1,0:T(8,128)} fusion(f32[7424,400]{1,0:T(8,128)} %copy.266, s32[1024]{0:T(1024)S(1)} %fusion.111), kind=kCustom, calls=%fused_computation.10.clone | custom fusion | bytes 3280896 | tf_op jit(solution)/shard_map/jit(_take)/gather | solution.py:50
  512.5 18.6 %all-gather.17.cloned.1.call-done = f32[2,512,400]{2,0,1:T(2,128)} async-done(((f32[2,32,400]{2,0,1:T(2,128)}), f32[2,512,400]{2,0,1:T(2,128)}) %all-gather.17.cloned.1.call-update) | async-done | bytes 1638416 | tf_op jit(solution)/shard_map/all_gather | solution.py:124
  531.2 5.0 fusion.145
  536.2 4.9 gather_fusion.6
  541.1 2.9 copy.287
  549.0 3.8 select_reduce_fusion.4
  553.6 4.2 fusion.42
  557.8 4.4 fusion.88
  562.1 3.5 gather_fusion.8
  577.8 18.1 %all-gather.3 = f32[8,2,32]{2,1,0:T(2,128)S(1)} all-gather(f32[1,2,32]{2,1,0:T(2,128)S(1)} %get-tuple-element.114), channel_id=1, replica_groups=mesh['bucket'=8,'dom'=16] {'bucket'}, dimensions={0}, use_global_device_ids=true | all-gather | bytes 2304 | tf_op jit(solution)/shard_map/all_gather | solution.py:104
  595.9 15.1 %all-gather.4 = f32[8,2,32]{2,1,0:T(2,128)S(1)} all-gather(f32[1,2,32]{2,1,0:T(2,128)S(1)} %bitcast.205), channel_id=1, replica_groups=mesh['bucket'=8,'dom'=16] {'bucket'}, dimensions={0}, use_global_device_ids=true | all-gather | bytes 2304 | tf_op jit(solution)/shard_map/all_gather | solution.py:93
  611.2 35.4 %reduce-scatter.17.cloned.1.call-done = f32[32,800]{1,0:T(8,128)} async-done(((f32[512,800]{1,0:T(8,128)}), f32[32,800]{1,0:T(8,128)}) %reduce-scatter.17.cloned.1.call-update) | async-done | bytes 102416 | tf_op jit(solution)/shard_map/reduce_scatter | solution.py:143
  647.8 32.7 %all_gather.58 = f32[16,32,400]{2,1,0:T(8,128)S(1)} all-gather(f32[2,32,400]{2,1,0:T(8,128)S(1)} %divide_subtract_fusion.1), channel_id=1, replica_groups=mesh['bucket'=8,'dom'=16] {'bucket'}, dimensions={0}, use_global_device_ids=true | all-gather | bytes 921600 | tf_op jit(solution)/shard_map/all_gather | solution.py:103
  681.8 3.9 all-to-all-start.5
  685.8 11.4 %all-to-all-done.5 = f32[8,2,32,400]{3,2,1,0:T(8,128)S(1)} async-done(((f32[8,2,32,400]{3,2,1,0:T(8,128)}), f32[8,2,32,400]{3,2,1,0:T(8,128)S(1)}, u32[]{:S(2)}, u32[]{:S(2)}) %all-to-all-start.5) | async-done | bytes 819232 | tf_op jit(solution)/shard_map/all_to_all | solution.py:13
  703.6 10.7 %gather_fusion.10 = f32[1024,400]{1,0:T(8,128)} fusion(f32[7424,400]{1,0:T(8,128)} %copy.266, s32[1024]{0:T(1024)S(1)} %fusion.114), kind=kCustom, calls=%fused_computation.11.clone | custom fusion | bytes 3280896 | tf_op jit(solution)/shard_map/jit(_take)/gather | solution.py:50
  719.9 24.2 %all-gather.19.cloned.1.call-done = f32[2,512,400]{2,0,1:T(2,128)} async-done(((f32[2,32,400]{2,0,1:T(2,128)}), f32[2,512,400]{2,0,1:T(2,128)}) %all-gather.19.cloned.1.call-update) | async-done | bytes 1638416 | tf_op jit(solution)/shard_map/all_gather | solution.py:124
  744.2 5.0 fusion.144
  749.3 4.9 gather_fusion.9
  754.2 2.9 copy.298
  762.1 3.8 select_reduce_fusion.1
  766.6 4.2 fusion.40
  770.8 4.4 fusion.85
  775.2 3.5 gather_fusion.11
  790.7 18.1 %all-gather.5 = f32[8,2,32]{2,1,0:T(2,128)S(1)} all-gather(f32[1,2,32]{2,1,0:T(2,128)S(1)} %get-tuple-element.112), channel_id=1, replica_groups=mesh['bucket'=8,'dom'=16] {'bucket'}, dimensions={0}, use_global_device_ids=true | all-gather | bytes 2304 | tf_op jit(solution)/shard_map/all_gather | solution.py:104
  808.9 15.1 %all-gather.6 = f32[8,2,32]{2,1,0:T(2,128)S(1)} all-gather(f32[1,2,32]{2,1,0:T(2,128)S(1)} %bitcast.206), channel_id=1, replica_groups=mesh['bucket'=8,'dom'=16] {'bucket'}, dimensions={0}, use_global_device_ids=true | all-gather | bytes 2304 | tf_op jit(solution)/shard_map/all_gather | solution.py:93
  824.1 35.4 %reduce-scatter.19.cloned.1.call-done = f32[32,800]{1,0:T(8,128)} async-done(((f32[512,800]{1,0:T(8,128)}), f32[32,800]{1,0:T(8,128)}) %reduce-scatter.19.cloned.1.call-update) | async-done | bytes 102416 | tf_op jit(solution)/shard_map/reduce_scatter | solution.py:143
  860.7 32.9 %all_gather.62 = f32[16,32,400]{2,1,0:T(8,128)S(1)} all-gather(f32[2,32,400]{2,1,0:T(8,128)S(1)} %divide_subtract_fusion), channel_id=1, replica_groups=mesh['bucket'=8,'dom'=16] {'bucket'}, dimensions={0}, use_global_device_ids=true | all-gather | bytes 921600 | tf_op jit(solution)/shard_map/all_gather | solution.py:103
  893.6 17.9 %all-gather.7 = f32[8,2,32]{2,1,0:T(2,128)S(1)} all-gather(f32[1,2,32]{2,1,0:T(2,128)S(1)} %get-tuple-element.110), channel_id=1, replica_groups=mesh['bucket'=8,'dom'=16] {'bucket'}, dimensions={0}, use_global_device_ids=true | all-gather | bytes 2304 | tf_op jit(solution)/shard_map/all_gather | solution.py:104
  (311 shorter events, 136.8 us)
Async XLA Ops:
  7.2 8.5 copy-start.47
  7.2 9.2 %copy-start.34 = (s32[4,8,2]{1,2,0:T(2,128)S(1)}, s32[4,8,2]{1,2,0:T(2,128)}, u32[]{:S(2)}) copy-start(s32[4,8,2]{1,2,0:T(2,128)} %param.14) | copy-start | bytes 772
  7.2 10.6 %copy-start.31 = (s32[4,1,1,16,512]{4,3,2,1,0:T(8,128)S(1)}, s32[4,1,1,16,512]{4,3,2,1,0:T(8,128)}, u32[]{:S(2)}) copy-start(s32[4,1,1,16,512]{4,3,2,1,0:T(8,128)} %param.17) | copy-start | bytes 393220
  9.2 35.6 %copy-start.33 = (s32[1,128,4,8,3]{1,3,4,2,0:T(8,128)S(1)}, s32[1,128,4,8,3]{1,3,4,2,0:T(8,128)}, u32[]{:S(2)}) copy-start(s32[1,128,4,8,3]{1,3,4,2,0:T(8,128)} %param.15) | copy-start | bytes 147460
  9.2 22.2 %all-to-all-start = ((f32[8,2,32,400]{3,2,1,0:T(8,128)}), f32[8,2,32,400]{3,2,1,0:T(8,128)S(1)}, u32[]{:S(2)}, u32[]{:S(2)}) async-start(f32[8,2,32,400]{3,2,1,0:T(8,128)} %stack.32), calls=%async_computation | async-start | bytes 2097152 | tf_op jit(solution)/shard_map/all_to_all | solution.py:13
  17.8 21.7 %copy-start.45 = (pred[2,16]{1,0:T(4,128)(4,1)}, pred[2,16]{1,0:T(4,128)(4,1)S(1)}, u32[]{:S(2)}) copy-start(pred[2,16]{1,0:T(4,128)(4,1)S(1)} %iota_compare_fusion.32) | copy-start | bytes 100
  31.4 32.2 %all-to-all-start.2 = ((s32[128,1,4]{2,1,0:T(1,128)}), s32[128,1,4]{2,1,0:T(1,128)S(1)}, u32[]{:S(2)}, u32[]{:S(2)}) async-start(s32[128,1,4]{2,1,0:T(1,128)} %bitcast.4), calls=%async_computation.2 | async-start | bytes 131072 | tf_op jit(solution)/shard_map/all_to_all | solution.py:116
  38.4 68.7 %all-gather.13.cloned.1.call-start = ((), (), s32[]{:S(2)}) async-start(), calls=%async_computation.10 | async-start | bytes 2228224 | tf_op jit(solution)/shard_map/all_gather | solution.py:124
  63.5 27.3 %all-to-all-start.1 = ((s32[128,4,8,3]{2,1,3,0:T(4,128)}), s32[128,4,8,3]{2,1,3,0:T(4,128)S(1)}, u32[]{:S(2)}, u32[]{:S(2)}) async-start(s32[128,4,8,3]{2,1,3,0:T(4,128)} %bitcast.1), calls=%async_computation.1 | async-start | bytes 1572864 | tf_op jit(solution)/shard_map/all_to_all | solution.py:115
  73.3 146.6 %reduce-scatter.13.cloned.1.call-start = ((), (), s32[]{:S(2)}) async-start(), calls=%async_computation.14 | async-start | bytes 1949696 | tf_op jit(solution)/shard_map/reduce_scatter | solution.py:143
  74.2 18.2 %copy-start.36 = (s32[128]{0:T(128)}, s32[128]{0:T(128)S(1)}, u32[]{:S(2)}) copy-start(s32[128]{0:T(128)S(1)} %get-tuple-element.6) | copy-start | bytes 1540
  119.9 1.9 copy-start.1
  121.9 1.9 copy-start
  121.9 2.4 copy-start.12
  145.3 1.4 copy-start.16
  147.0 2.5 copy-start.20
  147.0 2.5 copy-start.21
  151.5 2.4 copy-start.48
  151.5 17.6 %copy-start.46 = (pred[2,16]{1,0:T(4,128)(4,1)S(1)}, pred[2,16]{1,0:T(4,128)(4,1)}, u32[]{:S(2)}) copy-start(pred[2,16]{1,0:T(4,128)(4,1)} %copy-done.45) | copy-start | bytes 100
  169.8 86.0 %copy-start.39 = (pred[2,16]{1,0:T(4,128)(4,1)}, pred[2,16]{1,0:T(4,128)(4,1)S(1)}, u32[]{:S(2)}) copy-start(pred[2,16]{1,0:T(4,128)(4,1)S(1)} %get-tuple-element.129) | copy-start | bytes 100
  254.5 5.6 copy-start.51
  255.8 15.7 %all-to-all-start.3 = ((f32[8,2,32,400]{3,2,1,0:T(8,128)}), f32[8,2,32,400]{3,2,1,0:T(8,128)S(1)}, u32[]{:S(2)}, u32[]{:S(2)}) async-start(f32[8,2,32,400]{3,2,1,0:T(8,128)} %stack.36), calls=%async_computation.3 | async-start | bytes 2097152 | tf_op jit(solution)/shard_map/all_to_all | solution.py:13
  260.0 58.1 %all-gather.15.cloned.1.call-start = ((), (), s32[]{:S(2)}) async-start(), calls=%async_computation.11 | async-start | bytes 2228224 | tf_op jit(solution)/shard_map/all_gather | solution.py:124
  272.6 160.9 %reduce-scatter.15.cloned.1.call-start = ((), (), s32[]{:S(2)}) async-start(), calls=%async_computation.15 | async-start | bytes 1949696 | tf_op jit(solution)/shard_map/reduce_scatter | solution.py:143
  275.5 2.0 copy-start.37
  275.5 2.3 copy-start.30
  331.2 1.7 copy-start.13
  332.9 1.4 copy-start.2
  334.3 1.8 copy-start.8
  356.2 1.4 copy-start.3
  356.3 1.9 copy-start.17
  358.6 2.4 copy-start.22
  358.6 2.4 copy-start.23
  363.0 1.7 copy-start.42
  363.0 19.8 %copy-start.40 = (pred[2,16]{1,0:T(4,128)(4,1)S(1)}, pred[2,16]{1,0:T(4,128)(4,1)}, u32[]{:S(2)}) copy-start(pred[2,16]{1,0:T(4,128)(4,1)} %copy-done.39) | copy-start | bytes 100
  364.7 102.7 %copy-start.38 = (pred[2,16]{1,0:T(4,128)(4,1)S(1)}, pred[2,16]{1,0:T(4,128)(4,1)}, u32[]{:S(2)}) copy-start(pred[2,16]{1,0:T(4,128)(4,1)} %get-tuple-element.128) | copy-start | bytes 100
  467.3 5.5 copy-start.50
  468.7 16.7 %copy-start.43 = (s32[1,1,2]{1,2,0:T(2,128)S(1)}, s32[1,1,2]{1,2,0:T(2,128)}, u32[]{:S(2)}) copy-start(s32[1,1,2]{1,2,0:T(2,128)} %get-tuple-element.11) | copy-start | bytes 28
  468.7 16.7 %copy-start.44 = (s32[1,1,2]{1,2,0:T(2,128)S(1)}, s32[1,1,2]{1,2,0:T(2,128)}, u32[]{:S(2)}) copy-start(s32[1,1,2]{1,2,0:T(2,128)} %get-tuple-element.107) | copy-start | bytes 28
  468.7 18.7 %copy-start.32 = (s32[16,512]{1,0:T(8,128)S(1)}, s32[16,512]{1,0:T(8,128)}, u32[]{:S(2)}) copy-start(s32[16,512]{1,0:T(8,128)} %get-tuple-element.79) | copy-start | bytes 98308
  468.7 15.7 %all-to-all-start.4 = ((f32[8,2,32,400]{3,2,1,0:T(8,128)}), f32[8,2,32,400]{3,2,1,0:T(8,128)S(1)}, u32[]{:S(2)}, u32[]{:S(2)}) async-start(f32[8,2,32,400]{3,2,1,0:T(8,128)} %stack.40), calls=%async_computation.4 | async-start | bytes 2097152 | tf_op jit(solution)/shard_map/all_to_all | solution.py:13
  472.8 58.3 %all-gather.17.cloned.1.call-start = ((), (), s32[]{:S(2)}) async-start(), calls=%async_computation.12 | async-start | bytes 2228224 | tf_op jit(solution)/shard_map/all_gather | solution.py:124
  485.4 161.2 %reduce-scatter.17.cloned.1.call-start = ((), (), s32[]{:S(2)}) async-start(), calls=%async_computation.16 | async-start | bytes 1949696 | tf_op jit(solution)/shard_map/reduce_scatter | solution.py:143
  493.7 2.0 copy-start.35
  493.7 2.4 copy-start.29
  544.1 1.7 copy-start.14
  545.8 1.4 copy-start.4
  547.2 1.8 copy-start.9
  569.4 1.4 copy-start.5
  569.4 1.9 copy-start.18
  571.8 2.4 copy-start.24
  571.8 2.4 copy-start.25
  680.5 5.3 copy-start.49
  681.8 15.4 %all-to-all-start.5 = ((f32[8,2,32,400]{3,2,1,0:T(8,128)}), f32[8,2,32,400]{3,2,1,0:T(8,128)S(1)}, u32[]{:S(2)}, u32[]{:S(2)}) async-start(f32[8,2,32,400]{3,2,1,0:T(8,128)} %stack.44), calls=%async_computation.5 | async-start | bytes 2097152 | tf_op jit(solution)/shard_map/all_to_all | solution.py:13
  685.7 58.5 %all-gather.19.cloned.1.call-start = ((), (), s32[]{:S(2)}) async-start(), calls=%async_computation.13 | async-start | bytes 2228224 | tf_op jit(solution)/shard_map/all_gather | solution.py:124
  698.2 161.3 %reduce-scatter.19.cloned.1.call-start = ((), (), s32[]{:S(2)}) async-start(), calls=%async_computation.17 | async-start | bytes 1949696 | tf_op jit(solution)/shard_map/reduce_scatter | solution.py:143
  701.1 2.2 copy-start.28
  757.1 1.7 copy-start.15
  758.9 1.4 copy-start.6
  760.3 1.8 copy-start.10
  782.3 1.4 copy-start.7
  782.3 1.9 copy-start.19
  784.7 2.4 copy-start.26
  784.7 2.4 copy-start.27
  (6 other events, 6.2 us)
Sparse Core Ops, SparseCore 0:
  42.3 57.4 all-gather.12
  153.3 66.5 reduce-scatter.12
  272.7 45.3 all-gather.14
  364.8 68.5 reduce-scatter.14
  485.5 45.6 all-gather.16
  577.9 68.6 reduce-scatter.16
  698.3 45.7 all-gather.18
  790.9 68.6 reduce-scatter.18
